TPU v7x, 32 devices: a whole 2x2x4 slice. The times are simulated.
32 devices in a mesh: grp: 2 (over y), aux: 2 (over core), ao: 8 (over z, x).
Axes of the slice: x: 2, y: 2, z: 4, core: 2. Of those that a mesh axis runs over, the one named last changes fastest.
Arguments:
- blocks: bfloat16 [16, 2, 64, 64, 32], P(('grp', 'ao'), 'aux'), parts along dimension 0, may hold values from -6 to 6
- occ_density: bfloat16 [16, 64, 64], P(('grp', 'ao')), parts along dimension 0, may hold values from -0.0029296875 to 0.0029296875
- virt_density: bfloat16 [16, 64, 64], P(('grp', 'ao')), parts along dimension 0, may hold values from -0.75 to 0.75
- partner: int32 [16, 2], P(('grp', 'ao'), 'aux'), parts along dimension 0, may hold values from 0 to 7
- screen: int32 [16, 2], P(('grp', 'ao'), 'aux'), parts along dimension 0, may hold values 0 or 1
Outputs:
- chi: float32 [64, 32], P(('grp', 'aux', 'ao')), parts along dimension 0
There are 2 independent parts, one for each index of `grp`. A program takes and returns all parts, laid end to end along the dimension named above; each array names one. Nothing has to cross between parts.
Inputs may be any that keep to these rules, and one draw needn't show every extreme that they name: partner names an atom tile of its own part, an index into that part's 8 tiles.
All inputs are finite; a program needn't handle non-finite values. No bound on the sum of `screen` on one device may be relied on, other than what follows from the above.
Results may differ from a plain program's by a relative error of at most 0.0041.
Values may be sent and summed in bfloat16 or wider, within the bound.
A program may use at most 64 MiB of HBM per device.

v0:
```python
import jax
import jax.numpy as jnp
from jax import lax
from jax.sharding import PartitionSpec as P


def shards(blocks, occ_density, virt_density, partner, screen):
    tile_width = blocks.shape[2]
    aux_count = blocks.shape[4]
    target = partner[0, 0]
    gathered = lax.all_gather(virt_density, "ao", axis=0, tiled=True)
    chosen = lax.dynamic_index_in_dim(gathered, target, 0, keepdims=False)
    pair_block = blocks[0, 0]
    occ_side = jnp.dot(
        occ_density[0],
        pair_block.reshape(tile_width, tile_width * aux_count),
        preferred_element_type=jnp.float32,
    )
    occ_side = occ_side.astype(jnp.bfloat16).reshape(tile_width, tile_width, aux_count)
    dressed = jnp.einsum("mnp,nb->mbp", occ_side, chosen, preferred_element_type=jnp.float32)
    dressed = (dressed * screen[0, 0].astype(jnp.float32)).astype(jnp.bfloat16)
    dressed = dressed.reshape(tile_width * tile_width, aux_count)
    flat_block = pair_block.reshape(tile_width * tile_width, aux_count)
    chi_term = lax.dot_general(
        dressed, flat_block, (((0,), (0,)), ((), ())), preferred_element_type=jnp.float32
    )
    half_sum = lax.psum_scatter(chi_term, "aux", scatter_dimension=0, tiled=True)
    return lax.psum_scatter(half_sum, "ao", scatter_dimension=0, tiled=True)


def solution(mesh):
    placed = (
        P(("grp", "ao"), "aux", None, None, None),
        P(("grp", "ao"), None, None),
        P(("grp", "ao"), None, None),
        P(("grp", "ao"), "aux"),
        P(("grp", "ao"), "aux"),
    )
    return jax.shard_map(
        shards, mesh=mesh, in_specs=placed, out_specs=P(("grp", "aux", "ao"), None), check_vma=False
    )
```

profile of v0, /device:TPU:0, one launch (start us, length us, event | category | flops | bytes accessed | tf_op | source)
XLA Modules:
  0.0 83.8 jit_solution(6299920773656312131)
XLA Ops:
  6.5 0.0 copy-start
  6.5 0.0 copy-start.1
  6.5 0.0 reduce-scatter.2.cloned.1.call-start
  6.5 2.2 %copy.15 = bf16[1,1,64,64,32]{2,4,3,1,0:T(8,128)(2,1)S(1)} copy(bf16[1,1,64,64,32]{3,4,2,1,0:T(8,128)(2,1)} %param.5) | data formatting | bytes 524288 | tf_op args[0]
  8.7 0.0 copy-done.1
  8.8 0.2 copy.19
  9.6 0.0 copy-done
  9.6 0.3 convolution_convert_fusion
  9.9 0.0 copy-start.2
  9.9 0.3 copy.16
  10.2 0.4 copy-done.2
  10.7 32.3 %all_gather.3 = bf16[8,64,64]{2,1,0:T(8,128)(2,1)S(1)} all-gather(bf16[1,64,64]{2,1,0:T(8,128)(2,1)S(1)} %copy-done.2), channel_id=1, replica_groups=mesh['grp'=2,'aux'=2,'ao'=8] {'ao'}, dimensions={0}, use_global_device_ids=true | all-gather | bytes 73728 | tf_op jit(solution)/shard_map/all_gather | solution.py:11
  43.6 0.3 fusion.1
  44.0 0.3 copy.18
  44.2 0.5 reshape.8
  44.7 0.5 reshape_squeeze.7
  45.2 0.8 fusion.7
  46.0 0.0 reduce-scatter.2.cloned.1.call-update
  46.0 0.0 copy-start.3
  46.0 0.6 copy-done.3
  46.7 0.6 dynamic-slice
  47.9 6.6 %reduce-scatter.2.cloned.1.call-done = f32[16,32]{1,0:T(8,128)} async-done(((f32[32,32]{1,0:T(8,128)}), f32[16,32]{1,0:T(8,128)}) %reduce-scatter.2.cloned.1.call-update) | async-done | bytes 2064 | tf_op jit(solution)/shard_map/reduce_scatter | solution.py:27
  54.5 21.9 %all-reduce = f32[16,32]{1,0:T(8,128)S(1)} all-reduce(f32[16,32]{1,0:T(8,128)} %reduce-scatter.2.cloned.1.call-done), channel_id=3, replica_groups=mesh['grp'=2,'aux'=2,'ao'=8] {'ao'}, use_global_device_ids=true, to_apply=%region_1.2.clone | all-reduce | flops 512 | bytes 4096
  76.4 0.6 constant_dynamic-slice_fusion
Async XLA Ops:
  6.5 3.1 %copy-start = (bf16[1,64,64]{2,1,0:T(8,128)(2,1)S(1)}, bf16[1,64,64]{2,1,0:T(8,128)(2,1)}, u32[]{:S(2)}) copy-start(bf16[1,64,64]{2,1,0:T(8,128)(2,1)} %param.6) | copy-start | bytes 24580
  6.5 2.2 %copy-start.1 = (bf16[1,1,64,64,32]{3,4,2,1,0:T(8,128)(2,1)S(1)}, bf16[1,1,64,64,32]{3,4,2,1,0:T(8,128)(2,1)}, u32[]{:S(2)}) copy-start(bf16[1,1,64,64,32]{3,4,2,1,0:T(8,128)(2,1)} %param.5) | copy-start | bytes 786436
  6.5 47.9 %reduce-scatter.2.cloned.1.call-start = ((), (), s32[]{:S(2)}) async-start(), calls=%async_computation.1 | async-start | bytes 24576 | tf_op jit(solution)/shard_map/reduce_scatter | solution.py:27
  9.9 0.7 copy-start.2
  46.0 0.7 copy-start.3
Sparse Core Ops, SparseCore 0:
  46.1 8.3 reduce-scatter.1
where the time goes:
time: 84.1 us; the launch traced here: 83.8 us
  blocking collectives  54.2 us (64%)
  between operations  15.4 us (18%)
  waiting for transfers between devices  6.59 us (8%)
  local copies, waits for them, and re-layouts  6.13 us (7%)
  matrix products  1.46 us (2%)
    all_gather x1, blocking collectives, shards(): gathered = lax.all_gather(virt_density, 'ao', axis=0, tiled=True)  32.3 us
    unnamed x1, blocking collectives  21.9 us
    reduce_scatter x1, waiting for transfers between devices, shards(): lax.psum_scatter(chi_term, 'aux', scatter_dimension=0, tiled=True)  6.58 us
    unnamed x12, local copies, waits for them, and re-layouts  4.66 us
  transfers between devices with their start and end apart: 1, of which 1 were waited for; matrix products, arithmetic and copies ran while one was open for 1% of the time, Pallas kernels for 0%

commit v1 on v0

--- a/solution.py
+++ b/solution.py
@@ -1,10 +1,138 @@
+import functools
+
 import jax
 import jax.numpy as jnp
 from jax import lax
+from jax.experimental import pallas as pl
+from jax.experimental.pallas import tpu as pltpu
 from jax.sharding import PartitionSpec as P
 
+MESH = pl.DeviceIdType.MESH
+GROUP = 8
+KERNEL_ELEMENTS = 1 << 18
 
-def shards(blocks, occ_density, virt_density, partner, screen):
+
+def chi_kernel(aux_size, ao_size, blocks_hbm, occ_hbm, virt_hbm, partner_hbm, screen_hbm, chi_out,
+               pair, occ, virts, target, survives, outgoing, incoming,
+               load_sem, virt_send, virt_recv, chi_send, chi_recv):
+    width, aux_count = pair.shape[0], pair.shape[1]
+    devices = aux_size * ao_size
+    rows = aux_count // devices
+    my_aux, my_ao = lax.axis_index("aux"), lax.axis_index("ao")
+    me = my_aux * ao_size + my_ao
+
+    loads = [
+        pltpu.make_async_copy(blocks_hbm, pair, load_sem.at[0]),
+        pltpu.make_async_copy(occ_hbm.at[0], occ, load_sem.at[1]),
+        pltpu.make_async_copy(partner_hbm, target, load_sem.at[2]),
+        pltpu.make_async_copy(screen_hbm, survives, load_sem.at[3]),
+    ]
+    for load in loads:
+        load.start()
+    own_virt = pltpu.make_async_copy(virt_hbm.at[0], virts.at[my_ao], load_sem.at[4])
+    own_virt.start()
+
+    def peer(step):
+        other = lax.rem(me + step, devices)
+        return other, {"aux": lax.div(other, ao_size), "ao": lax.rem(other, ao_size)}
+
+    barrier = pltpu.get_barrier_semaphore()
+    for step in range(1, devices):
+        pl.semaphore_signal(barrier, inc=1, device_id=peer(step)[1], device_id_type=MESH)
+    pl.semaphore_wait(barrier, devices - 1)
+
+    virt_copies = []
+    for step in range(1, ao_size):
+        copy = pltpu.make_async_remote_copy(
+            src_ref=virt_hbm.at[0], dst_ref=virts.at[my_ao],
+            send_sem=virt_send.at[step - 1], recv_sem=virt_recv.at[step - 1],
+            device_id={"ao": lax.rem(my_ao + step, ao_size)}, device_id_type=MESH)
+        copy.start()
+        virt_copies.append(copy)
+
+    for load in loads:
+        load.wait()
+    stack = pair[...]
+    by_aux = jnp.swapaxes(stack.astype(jnp.float32), 0, 1).astype(jnp.bfloat16)
+    occ_block = occ[...]
+    left = jnp.stack([
+        jnp.dot(occ_block, by_aux[index], preferred_element_type=jnp.float32)
+        for index in range(aux_count)
+    ])
+    left = jnp.swapaxes(left, 0, 1).astype(jnp.bfloat16).reshape(width * aux_count, width)
+
+    own_virt.wait()
+    for copy in virt_copies:
+        copy.wait()
+    chosen = virts[target[0, 0]]
+    flat = stack.reshape(width * aux_count, width)
+    right = lax.dot_general(flat, chosen, (((1,), (1,)), ((), ())), preferred_element_type=jnp.float32)
+    right = right.astype(jnp.bfloat16)
+
+    span = GROUP * aux_count
+    gram = jnp.zeros((span, span), jnp.float32)
+    for start in range(0, width * aux_count, span):
+        gram += lax.dot_general(left[start:start + span], right[start:start + span],
+                                (((1,), (1,)), ((), ())), preferred_element_type=jnp.float32)
+    lane = lax.broadcasted_iota(jnp.int32, (aux_count, span), 1)
+    wide = jnp.zeros((aux_count, span), jnp.float32)
+    for index in range(GROUP):
+        low = index * aux_count
+        wide = jnp.where((lane >= low) & (lane < low + aux_count), gram[low:low + aux_count], wide)
+    chi = wide[:, :aux_count]
+    for index in range(1, GROUP):
+        chi += wide[:, index * aux_count:(index + 1) * aux_count]
+    chi = chi * survives[0, 0].astype(jnp.float32)
+
+    for index in range(devices):
+        outgoing[index] = chi[index * rows:(index + 1) * rows]
+    chi_copies = []
+    for step in range(1, devices):
+        other, device = peer(step)
+        copy = pltpu.make_async_remote_copy(
+            src_ref=outgoing.at[other], dst_ref=incoming.at[me],
+            send_sem=chi_send.at[step - 1], recv_sem=chi_recv.at[step - 1],
+            device_id=device, device_id_type=MESH)
+        copy.start()
+        chi_copies.append(copy)
+    incoming[me] = outgoing[me]
+    for copy in chi_copies:
+        copy.wait()
+    chi_out[...] = jnp.sum(incoming[...], axis=0)
+
+
+def fused_shards(aux_size, ao_size, blocks, occ_density, virt_density, partner, screen):
+    width, aux_count = blocks.shape[2], blocks.shape[4]
+    devices = aux_size * ao_size
+    rows = aux_count // devices
+    pair = jnp.swapaxes(blocks[0, 0], 1, 2)
+    hbm = pl.BlockSpec(memory_space=pl.ANY)
+    return pl.pallas_call(
+        functools.partial(chi_kernel, aux_size, ao_size),
+        out_shape=jax.ShapeDtypeStruct((rows, aux_count), jnp.float32),
+        in_specs=[hbm] * 5,
+        out_specs=pl.BlockSpec(memory_space=pltpu.VMEM),
+        scratch_shapes=[
+            pltpu.VMEM((width, aux_count, width), jnp.bfloat16),
+            pltpu.VMEM((width, width), jnp.bfloat16),
+            pltpu.VMEM((ao_size, width, width), jnp.bfloat16),
+            pltpu.SMEM((1, 1), jnp.int32),
+            pltpu.SMEM((1, 1), jnp.int32),
+            pltpu.VMEM((devices, rows, aux_count), jnp.float32),
+            pltpu.VMEM((devices, rows, aux_count), jnp.float32),
+            pltpu.SemaphoreType.DMA((5,)),
+            pltpu.SemaphoreType.DMA((ao_size - 1,)),
+            pltpu.SemaphoreType.DMA((ao_size - 1,)),
+            pltpu.SemaphoreType.DMA((devices - 1,)),
+            pltpu.SemaphoreType.DMA((devices - 1,)),
+        ],
+        compiler_params=pltpu.CompilerParams(
+            collective_id=0, has_side_effects=True, vmem_limit_bytes=32 << 20
+        ),
+    )(pair, occ_density, virt_density, partner, screen)
+
+
+def staged_shards(blocks, occ_density, virt_density, partner, screen):
     tile_width = blocks.shape[2]
     aux_count = blocks.shape[4]
     target = partner[0, 0]
@@ -29,6 +157,7 @@
 
 
 def solution(mesh):
+    aux_size, ao_size = mesh.shape["aux"], mesh.shape["ao"]
     placed = (
         P(("grp", "ao"), "aux", None, None, None),
         P(("grp", "ao"), None, None),
@@ -36,6 +165,12 @@
         P(("grp", "ao"), "aux"),
         P(("grp", "ao"), "aux"),
     )
+
+    def shards(blocks, *rest):
+        if blocks.size <= KERNEL_ELEMENTS:
+            return fused_shards(aux_size, ao_size, blocks, *rest)
+        return staged_shards(blocks, *rest)
+
     return jax.shard_map(
         shards, mesh=mesh, in_specs=placed, out_specs=P(("grp", "aux", "ao"), None), check_vma=False
     )

time: 84.1 us -> 21.5 us (0.26)
  blocking collectives: 54.2 us -> 0 us
  Pallas kernels: 0 us -> 16.8 us
  between operations: 15.4 us -> 1.32 us
  waiting for transfers between devices: 6.59 us -> 0 us
  local copies, waits for them, and re-layouts: 6.13 us -> 3.03 us
  matrix products: 1.46 us -> 0 us
    all_gather x1 -> x0, blocking collectives: 32.3 us -> none  [shards(): gathered = lax.all_gather(virt_density, 'ao', axis=0, tiled=True)]
    unnamed x1 -> x0, blocking collectives: 21.9 us -> none
    pallas_call x0 -> x1, Pallas kernels: none -> 16.8 us  [fused_shards(): pl.pallas_call(functools.partial(chi_kernel, aux_size, ao_size), out_shap...]
    reduce_scatter x1 -> x0, waiting for transfers between devices: 6.58 us -> none  [shards(): lax.psum_scatter(chi_term, 'aux', scatter_dimension=0, tiled=True)]
    unnamed x12 -> x7, local copies, waits for them, and re-layouts: 4.66 us -> 3.03 us
    dot_general x3 -> x0, matrix products: 1.46 us -> none  [the longest x1 0.82 us: shards(): lax.dot_general(dressed, flat_block, (((0,), (0,)), ((), ())), preferred_...]
  transfers between devices with their start and end apart: 1 -> 0, of which waited for: 1 -> 0; matrix products, arithmetic and copies ran while one was open for 1% -> 0% of each run, Pallas kernels for 0% -> 0%
where the time goes in v1:
time: 21.5 us; the launch traced here: 21.1 us
  Pallas kernels  16.8 us (78%)
  local copies, waits for them, and re-layouts  3.03 us (14%)
  between operations  1.32 us (6%)
    pallas_call x1, Pallas kernels, fused_shards(): pl.pallas_call(functools.partial(chi_kernel, aux_size, ao_size), out_shap...  16.8 us
    unnamed x7, local copies, waits for them, and re-layouts  3.03 us

profile of v1, /device:TPU:0, one launch (start us, length us, event | category | flops | bytes accessed | tf_op | source)
XLA Modules:
  0.0 21.1 jit_solution(4955455276965995984)
XLA Ops:
  1.3 0.0 copy-start
  1.3 1.0 %copy-done = bf16[1,1,64,64,32]{3,4,2,1,0:T(8,128)(2,1)S(1)} copy-done((bf16[1,1,64,64,32]{3,4,2,1,0:T(8,128)(2,1)S(1)}, bf16[1,1,64,64,32]{3,4,2,1,0:T(8,128)(2,1)}, u32[]{:S(2)}) %copy-start) | copy-done | bytes 262168
  2.3 0.0 copy-start.1
  2.3 0.7 %copy-done.1 = bf16[1,64,64]{2,1,0:T(8,128)(2,1)S(1)} copy-done((bf16[1,64,64]{2,1,0:T(8,128)(2,1)S(1)}, bf16[1,64,64]{2,1,0:T(8,128)(2,1)}, u32[]{:S(2)}) %copy-start.1) | copy-done | bytes 8216
  3.1 0.0 copy-start.2
  3.1 0.7 %copy-done.2 = bf16[1,64,64]{2,1,0:T(8,128)(2,1)S(1)} copy-done((bf16[1,64,64]{2,1,0:T(8,128)(2,1)S(1)}, bf16[1,64,64]{2,1,0:T(8,128)(2,1)}, u32[]{:S(2)}) %copy-start.2) | copy-done | bytes 8216
  3.8 16.8 %shard_map.55 = f32[2,32]{1,0:T(2,128)S(1)} custom-call(bf16[64,32,64]{2,1,0:T(8,128)(2,1)S(1)} %bitcast.3, bf16[1,64,64]{2,1,0:T(8,128)(2,1)S(1)} %copy-done.1, bf16[1,64,64]{2,1,0:T(8,128)(2,1)S(1)} %copy-done.2, s32[1,1]{1,0:T(1,128)S(6)} %copy.7.partner_hbm, s32[1,1]{1,0:T(1,128)S(6)} %copy.8.screen_hbm), custom_call_target="tpu_custom_call" | custom-call | tf_op jit(solution)/shard_map/pallas_call | solution.py:110
  20.6 0.6 %copy.9 = f32[2,32]{1,0:T(2,128)} copy(f32[2,32]{1,0:T(2,128)S(1)} %shard_map.55) | data formatting | bytes 512
Async XLA Ops:
  1.3 1.0 %copy-start = (bf16[1,1,64,64,32]{3,4,2,1,0:T(8,128)(2,1)S(1)}, bf16[1,1,64,64,32]{3,4,2,1,0:T(8,128)(2,1)}, u32[]{:S(2)}) copy-start(bf16[1,1,64,64,32]{3,4,2,1,0:T(8,128)(2,1)} %param.5) | copy-start | bytes 786436
  2.3 0.7 %copy-start.1 = (bf16[1,64,64]{2,1,0:T(8,128)(2,1)S(1)}, bf16[1,64,64]{2,1,0:T(8,128)(2,1)}, u32[]{:S(2)}) copy-start(bf16[1,64,64]{2,1,0:T(8,128)(2,1)} %occ_hbm.1) | copy-start | bytes 24580
  3.1 0.7 %copy-start.2 = (bf16[1,64,64]{2,1,0:T(8,128)(2,1)S(1)}, bf16[1,64,64]{2,1,0:T(8,128)(2,1)}, u32[]{:S(2)}) copy-start(bf16[1,64,64]{2,1,0:T(8,128)(2,1)} %virt_hbm.1) | copy-start | bytes 24580

commit v2 on v1

--- a/solution.py
+++ b/solution.py
@@ -12,8 +12,17 @@
 KERNEL_ELEMENTS = 1 << 18
 
 
+def flipped(position, mask, count):
+    other, bit = position, 1
+    while bit < count:
+        if mask & bit:
+            other = other + (1 - 2 * lax.rem(lax.div(position, bit), 2)) * bit
+        bit *= 2
+    return other
+
+
 def chi_kernel(aux_size, ao_size, blocks_hbm, occ_hbm, virt_hbm, partner_hbm, screen_hbm, chi_out,
-               pair, occ, virts, target, survives, outgoing, incoming,
+               pair, occ, own_virt, virts, target, survives, outgoing, incoming,
                load_sem, virt_send, virt_recv, chi_send, chi_recv):
     width, aux_count = pair.shape[0], pair.shape[1]
     devices = aux_size * ao_size
@@ -21,6 +30,19 @@
     my_aux, my_ao = lax.axis_index("aux"), lax.axis_index("ao")
     me = my_aux * ao_size + my_ao
 
+    peers = []
+    for ao_mask in range(ao_size - 1, -1, -1):
+        for aux_mask in range(aux_size - 1, -1, -1):
+            if ao_mask or aux_mask:
+                aux, ao = flipped(my_aux, aux_mask, aux_size), flipped(my_ao, ao_mask, ao_size)
+                peers.append((aux * ao_size + ao, {"aux": aux, "ao": ao}))
+
+    barrier = pltpu.get_barrier_semaphore()
+    for _, device in peers:
+        pl.semaphore_signal(barrier, inc=1, device_id=device, device_id_type=MESH)
+
+    virt_load = pltpu.make_async_copy(virt_hbm.at[0], own_virt, load_sem.at[4])
+    virt_load.start()
     loads = [
         pltpu.make_async_copy(blocks_hbm, pair, load_sem.at[0]),
         pltpu.make_async_copy(occ_hbm.at[0], occ, load_sem.at[1]),
@@ -29,24 +51,17 @@
     ]
     for load in loads:
         load.start()
-    own_virt = pltpu.make_async_copy(virt_hbm.at[0], virts.at[my_ao], load_sem.at[4])
-    own_virt.start()
+    half = width // 2
+    virt_load.wait()
+    virts[my_ao] = jnp.concatenate([own_virt[:half], own_virt[half:]], axis=1)
 
-    def peer(step):
-        other = lax.rem(me + step, devices)
-        return other, {"aux": lax.div(other, ao_size), "ao": lax.rem(other, ao_size)}
-
-    barrier = pltpu.get_barrier_semaphore()
-    for step in range(1, devices):
-        pl.semaphore_signal(barrier, inc=1, device_id=peer(step)[1], device_id_type=MESH)
     pl.semaphore_wait(barrier, devices - 1)
-
     virt_copies = []
-    for step in range(1, ao_size):
+    for ao_mask in range(ao_size - 1, 0, -1):
         copy = pltpu.make_async_remote_copy(
-            src_ref=virt_hbm.at[0], dst_ref=virts.at[my_ao],
-            send_sem=virt_send.at[step - 1], recv_sem=virt_recv.at[step - 1],
-            device_id={"ao": lax.rem(my_ao + step, ao_size)}, device_id_type=MESH)
+            src_ref=virts.at[my_ao], dst_ref=virts.at[my_ao],
+            send_sem=virt_send.at[ao_mask - 1], recv_sem=virt_recv.at[ao_mask - 1],
+            device_id={"ao": flipped(my_ao, ao_mask, ao_size)}, device_id_type=MESH)
         copy.start()
         virt_copies.append(copy)
 
@@ -61,10 +76,10 @@
     ])
     left = jnp.swapaxes(left, 0, 1).astype(jnp.bfloat16).reshape(width * aux_count, width)
 
-    own_virt.wait()
-    for copy in virt_copies:
-        copy.wait()
+    for copy in reversed(virt_copies):
+        copy.wait_recv()
     chosen = virts[target[0, 0]]
+    chosen = jnp.concatenate([chosen[:, :width], chosen[:, width:]], axis=0)
     flat = stack.reshape(width * aux_count, width)
     right = lax.dot_general(flat, chosen, (((1,), (1,)), ((), ())), preferred_element_type=jnp.float32)
     right = right.astype(jnp.bfloat16)
@@ -87,17 +102,18 @@
     for index in range(devices):
         outgoing[index] = chi[index * rows:(index + 1) * rows]
     chi_copies = []
-    for step in range(1, devices):
-        other, device = peer(step)
+    for index, (other, device) in enumerate(peers):
         copy = pltpu.make_async_remote_copy(
             src_ref=outgoing.at[other], dst_ref=incoming.at[me],
-            send_sem=chi_send.at[step - 1], recv_sem=chi_recv.at[step - 1],
+            send_sem=chi_send.at[index], recv_sem=chi_recv.at[index],
             device_id=device, device_id_type=MESH)
         copy.start()
         chi_copies.append(copy)
     incoming[me] = outgoing[me]
-    for copy in chi_copies:
-        copy.wait()
+    for copy in virt_copies + chi_copies:
+        copy.wait_send()
+    for copy in reversed(chi_copies):
+        copy.wait_recv()
     chi_out[...] = jnp.sum(incoming[...], axis=0)
 
 
@@ -115,7 +131,8 @@
         scratch_shapes=[
             pltpu.VMEM((width, aux_count, width), jnp.bfloat16),
             pltpu.VMEM((width, width), jnp.bfloat16),
-            pltpu.VMEM((ao_size, width, width), jnp.bfloat16),
+            pltpu.VMEM((width, width), jnp.bfloat16),
+            pltpu.VMEM((ao_size, width // 2, 2 * width), jnp.bfloat16),
             pltpu.SMEM((1, 1), jnp.int32),
             pltpu.SMEM((1, 1), jnp.int32),
             pltpu.VMEM((devices, rows, aux_count), jnp.float32),
@@ -127,7 +144,7 @@
             pltpu.SemaphoreType.DMA((devices - 1,)),
         ],
         compiler_params=pltpu.CompilerParams(
-            collective_id=0, has_side_effects=True, vmem_limit_bytes=32 << 20
+            collective_id=0, has_side_effects=True, vmem_limit_bytes=60 << 20
         ),
     )(pair, occ_density, virt_density, partner, screen)
 
@@ -166,8 +183,10 @@
         P(("grp", "ao"), "aux"),
     )
 
+    devices = aux_size * ao_size
+
     def shards(blocks, *rest):
-        if blocks.size <= KERNEL_ELEMENTS:
+        if blocks.size <= KERNEL_ELEMENTS and devices & (devices - 1) == 0:
             return fused_shards(aux_size, ao_size, blocks, *rest)
         return staged_shards(blocks, *rest)
 

time: 21.5 us -> 18.7 us (0.87)
  local copies, waits for them, and re-layouts: 3.03 us -> 1.24 us
  Pallas kernels: 16.8 us -> 15.9 us
    unnamed x7 -> x1, local copies, waits for them, and re-layouts: 3.03 us -> 1.24 us
    pallas_call x1, Pallas kernels: 16.8 us -> 15.9 us  [fused_shards(): pl.pallas_call(functools.partial(chi_kernel, aux_size, ao_size), out_shap...]
where the time goes in v2:
time: 18.7 us; the launch traced here: 18.5 us
  Pallas kernels  15.9 us (85%)
  between operations  1.3 us (7%)
  local copies, waits for them, and re-layouts  1.24 us (7%)
    pallas_call x1, Pallas kernels, fused_shards(): pl.pallas_call(functools.partial(chi_kernel, aux_size, ao_size), out_shap...  15.9 us
    unnamed x1, local copies, waits for them, and re-layouts  1.24 us

profile of v2, /device:TPU:0, one launch (start us, length us, event | category | flops | bytes accessed | tf_op | source)
XLA Modules:
  0.0 18.5 jit_solution(11731316658038417019)
XLA Ops:
  1.3 15.9 %shard_map.55 = f32[2,32]{1,0:T(2,128)} custom-call(bf16[64,32,64]{2,1,0:T(8,128)(2,1)} %bitcast.3, bf16[1,64,64]{2,1,0:T(8,128)(2,1)} %occ_hbm.1, bf16[1,64,64]{2,1,0:T(8,128)(2,1)} %virt_hbm.1, s32[1,1]{1,0:T(1,128)S(6)} %copy.7.partner_hbm, s32[1,1]{1,0:T(1,128)S(6)} %copy.8.screen_hbm), custom_call_target="tpu_custom_call" | custom-call | tf_op jit(solution)/shard_map/pallas_call | solution.py:126
  17.2 1.2 %copy.9 = f32[2,32]{1,0:T(2,128)} copy(f32[2,32]{1,0:T(2,128)} %shard_map.55) | data formatting | bytes 512

commit v3 on v2

--- a/solution.py
+++ b/solution.py
@@ -21,8 +21,8 @@
     return other
 
 
-def chi_kernel(aux_size, ao_size, blocks_hbm, occ_hbm, virt_hbm, partner_hbm, screen_hbm, chi_out,
-               pair, occ, own_virt, virts, target, survives, outgoing, incoming,
+def chi_kernel(aux_size, ao_size, blocks_hbm, occ_hbm, virt_hbm, partner_hbm, screen_hbm, incoming,
+               pair, occ, own_virt, virts, target, survives, outgoing,
                load_sem, virt_send, virt_recv, chi_send, chi_recv):
     width, aux_count = pair.shape[0], pair.shape[1]
     devices = aux_size * ao_size
@@ -114,7 +114,6 @@
         copy.wait_send()
     for copy in reversed(chi_copies):
         copy.wait_recv()
-    chi_out[...] = jnp.sum(incoming[...], axis=0)
 
 
 def fused_shards(aux_size, ao_size, blocks, occ_density, virt_density, partner, screen):
@@ -123,9 +122,9 @@
     rows = aux_count // devices
     pair = jnp.swapaxes(blocks[0, 0], 1, 2)
     hbm = pl.BlockSpec(memory_space=pl.ANY)
-    return pl.pallas_call(
+    terms = pl.pallas_call(
         functools.partial(chi_kernel, aux_size, ao_size),
-        out_shape=jax.ShapeDtypeStruct((rows, aux_count), jnp.float32),
+        out_shape=pltpu.VMEM((devices, rows, aux_count), jnp.float32),
         in_specs=[hbm] * 5,
         out_specs=pl.BlockSpec(memory_space=pltpu.VMEM),
         scratch_shapes=[
@@ -135,7 +134,6 @@
             pltpu.VMEM((ao_size, width // 2, 2 * width), jnp.bfloat16),
             pltpu.SMEM((1, 1), jnp.int32),
             pltpu.SMEM((1, 1), jnp.int32),
-            pltpu.VMEM((devices, rows, aux_count), jnp.float32),
             pltpu.VMEM((devices, rows, aux_count), jnp.float32),
             pltpu.SemaphoreType.DMA((5,)),
             pltpu.SemaphoreType.DMA((ao_size - 1,)),
@@ -147,6 +145,7 @@
             collective_id=0, has_side_effects=True, vmem_limit_bytes=60 << 20
         ),
     )(pair, occ_density, virt_density, partner, screen)
+    return jnp.sum(terms, axis=0)
 
 
 def staged_shards(blocks, occ_density, virt_density, partner, screen):

time: 18.7 us -> 17.4 us (0.930)
  local copies, waits for them, and re-layouts: 1.24 us -> 0 us
  Pallas kernels: 15.9 us -> 15.3 us
  other arithmetic: 0 us -> 0.59 us
    unnamed x1 -> x0, local copies, waits for them, and re-layouts: 1.24 us -> none
    pallas_call x1, Pallas kernels: 15.9 us -> 15.3 us  [fused_shards(): pl.pallas_call(functools.partial(chi_kernel, aux_size, ao_size), out_shap...]
    reduce_sum x0 -> x1, other arithmetic: none -> 0.59 us  [fused_shards(): return jnp.sum(terms, axis=0)]
where the time goes in v3:
time: 17.4 us; the launch traced here: 17.2 us
  Pallas kernels  15.3 us (88%)
  between operations  1.3 us (7%)
  other arithmetic  0.59 us (3%)
    pallas_call x1, Pallas kernels, fused_shards(): pl.pallas_call(functools.partial(chi_kernel, aux_size, ao_size), out_shap...  15.3 us
    reduce_sum x1, other arithmetic, fused_shards(): return jnp.sum(terms, axis=0)  0.59 us

profile of v3, /device:TPU:0, one launch (start us, length us, event | category | flops | bytes accessed | tf_op | source)
XLA Modules:
  0.0 17.2 jit_solution(15672196990056857759)
XLA Ops:
  1.3 15.3 %shard_map.55 = f32[16,2,32]{2,1,0:T(2,128)S(1)} custom-call(bf16[64,32,64]{2,1,0:T(8,128)(2,1)} %bitcast.3, bf16[1,64,64]{2,1,0:T(8,128)(2,1)} %occ_hbm.1, bf16[1,64,64]{2,1,0:T(8,128)(2,1)} %virt_hbm.1, s32[1,1]{1,0:T(1,128)S(6)} %copy.6.partner_hbm, s32[1,1]{1,0:T(1,128)S(6)} %copy.7.screen_hbm), custom_call_target="tpu_custom_call" | custom-call | tf_op jit(solution)/shard_map/pallas_call | solution.py:125
  16.6 0.6 %reduce_sum.9 = f32[2,32]{1,0:T(2,128)} reduce(f32[16,2,32]{2,1,0:T(2,128)S(1)} %shard_map.55, f32[]{:T(128)} %constant.0.clone.1), dimensions={0}, to_apply=%region_0.0 | reduce | flops 960 | bytes 4356 | tf_op jit(solution)/shard_map/reduce_sum | solution.py:148

commit v4 on v3

--- a/solution.py
+++ b/solution.py
@@ -9,6 +9,7 @@
 
 MESH = pl.DeviceIdType.MESH
 GROUP = 8
+PACK = 4
 KERNEL_ELEMENTS = 1 << 18
 
 
@@ -19,6 +20,11 @@
             other = other + (1 - 2 * lax.rem(lax.div(position, bit), 2)) * bit
         bit *= 2
     return other
+
+
+def packed(rows):
+    run = rows.shape[0] // PACK
+    return jnp.concatenate([rows[index * run:(index + 1) * run] for index in range(PACK)], axis=1)
 
 
 def chi_kernel(aux_size, ao_size, blocks_hbm, occ_hbm, virt_hbm, partner_hbm, screen_hbm, incoming,
@@ -74,19 +80,23 @@
         jnp.dot(occ_block, by_aux[index], preferred_element_type=jnp.float32)
         for index in range(aux_count)
     ])
-    left = jnp.swapaxes(left, 0, 1).astype(jnp.bfloat16).reshape(width * aux_count, width)
+    left = packed(jnp.swapaxes(left, 0, 1).astype(jnp.bfloat16).reshape(width * aux_count, width))
+    flat = packed(stack.reshape(width * aux_count, width))
 
     for copy in reversed(virt_copies):
         copy.wait_recv()
     chosen = virts[target[0, 0]]
     chosen = jnp.concatenate([chosen[:, :width], chosen[:, width:]], axis=0)
-    flat = stack.reshape(width * aux_count, width)
-    right = lax.dot_general(flat, chosen, (((1,), (1,)), ((), ())), preferred_element_type=jnp.float32)
+    chosen = jnp.concatenate([chosen] * PACK, axis=1)
+    side = lax.div(lax.broadcasted_iota(jnp.int32, chosen.shape, 1), width)
+    blank = jnp.zeros_like(chosen)
+    diagonal = jnp.concatenate([jnp.where(side == index, chosen, blank) for index in range(PACK)], axis=0)
+    right = lax.dot_general(flat, diagonal, (((1,), (1,)), ((), ())), preferred_element_type=jnp.float32)
     right = right.astype(jnp.bfloat16)
 
     span = GROUP * aux_count
     gram = jnp.zeros((span, span), jnp.float32)
-    for start in range(0, width * aux_count, span):
+    for start in range(0, flat.shape[0], span):
         gram += lax.dot_general(left[start:start + span], right[start:start + span],
                                 (((1,), (1,)), ((), ())), preferred_element_type=jnp.float32)
     lane = lax.broadcasted_iota(jnp.int32, (aux_count, span), 1)

time: 17.4 us -> 17.3 us (level)
  no operation moved by 1% of the time
where the time goes in v4:
time: 17.3 us; the launch traced here: 17.1 us
  Pallas kernels  15.2 us (88%)
  between operations  1.3 us (8%)
  other arithmetic  0.59 us (3%)
    pallas_call x1, Pallas kernels, fused_shards(): pl.pallas_call(functools.partial(chi_kernel, aux_size, ao_size), out_shap...  15.2 us
    reduce_sum x1, other arithmetic, fused_shards(): return jnp.sum(terms, axis=0)  0.59 us

profile of v4, /device:TPU:0, one launch (start us, length us, event | category | flops | bytes accessed | tf_op | source)
XLA Modules:
  0.0 17.1 jit_solution(116158387003501292)
XLA Ops:
  1.3 15.2 %shard_map.55 = f32[16,2,32]{2,1,0:T(2,128)S(1)} custom-call(bf16[64,32,64]{2,1,0:T(8,128)(2,1)} %bitcast.3, bf16[1,64,64]{2,1,0:T(8,128)(2,1)} %occ_hbm.1, bf16[1,64,64]{2,1,0:T(8,128)(2,1)} %virt_hbm.1, s32[1,1]{1,0:T(1,128)S(6)} %copy.6.partner_hbm, s32[1,1]{1,0:T(1,128)S(6)} %copy.7.screen_hbm), custom_call_target="tpu_custom_call" | custom-call | tf_op jit(solution)/shard_map/pallas_call | solution.py:135
  16.5 0.6 %reduce_sum.9 = f32[2,32]{1,0:T(2,128)} reduce(f32[16,2,32]{2,1,0:T(2,128)S(1)} %shard_map.55, f32[]{:T(128)} %constant.0.clone.1), dimensions={0}, to_apply=%region_0.0 | reduce | flops 960 | bytes 4356 | tf_op jit(solution)/shard_map/reduce_sum | solution.py:158

commit v5 on v4

--- a/solution.py
+++ b/solution.py
@@ -104,9 +104,10 @@
     for index in range(GROUP):
         low = index * aux_count
         wide = jnp.where((lane >= low) & (lane < low + aux_count), gram[low:low + aux_count], wide)
-    chi = wide[:, :aux_count]
-    for index in range(1, GROUP):
-        chi += wide[:, index * aux_count:(index + 1) * aux_count]
+    chi = wide
+    while chi.shape[1] > aux_count:
+        middle = chi.shape[1] // 2
+        chi = chi[:, :middle] + chi[:, middle:]
     chi = chi * survives[0, 0].astype(jnp.float32)
 
     for index in range(devices):

time: 17.3 us -> 17.4 us (level)
  no operation moved by 1% of the time
where the time goes in v5:
time: 17.4 us; the launch traced here: 17.1 us
  Pallas kernels  15.2 us (87%)
  between operations  1.3 us (7%)
  other arithmetic  0.59 us (3%)
    pallas_call x1, Pallas kernels, fused_shards(): pl.pallas_call(functools.partial(chi_kernel, aux_size, ao_size), out_shap...  15.2 us
    reduce_sum x1, other arithmetic, fused_shards(): return jnp.sum(terms, axis=0)  0.59 us

profile of v5, /device:TPU:0, one launch (start us, length us, event | category | flops | bytes accessed | tf_op | source)
XLA Modules:
  0.0 17.1 jit_solution(6631775447641117887)
XLA Ops:
  1.3 15.2 %shard_map.55 = f32[16,2,32]{2,1,0:T(2,128)S(1)} custom-call(bf16[64,32,64]{2,1,0:T(8,128)(2,1)} %bitcast.3, bf16[1,64,64]{2,1,0:T(8,128)(2,1)} %occ_hbm.1, bf16[1,64,64]{2,1,0:T(8,128)(2,1)} %virt_hbm.1, s32[1,1]{1,0:T(1,128)S(6)} %copy.6.partner_hbm, s32[1,1]{1,0:T(1,128)S(6)} %copy.7.screen_hbm), custom_call_target="tpu_custom_call" | custom-call | tf_op jit(solution)/shard_map/pallas_call | solution.py:136
  16.5 0.6 %reduce_sum.9 = f32[2,32]{1,0:T(2,128)} reduce(f32[16,2,32]{2,1,0:T(2,128)S(1)} %shard_map.55, f32[]{:T(128)} %constant.0.clone.1), dimensions={0}, to_apply=%region_0.0 | reduce | flops 960 | bytes 4356 | tf_op jit(solution)/shard_map/reduce_sum | solution.py:159
